TPU v7x, 128 devices: a whole 4x4x4 slice. The times are simulated.
128 devices in a mesh: tile: 8 (over z, x_hi), head: 8 (over y, x_lo), dp: 2 (over core).
Axes of the slice: x: 4 (x_hi: 2, x_lo: 2; x = x_hi * 2 + x_lo), y: 4, z: 4, core: 2. Of those that a mesh axis runs over, the one named last changes fastest.
Arguments:
- queries: bfloat16 [2, 12288, 3072], P('dp', ('tile', 'head')), may hold values from -24 to 24
- keys: bfloat16 [2, 12288, 3072], P('dp', ('tile', 'head')), may hold values from -24 to 24
- values: bfloat16 [2, 12288, 3072], P('dp', ('tile', 'head')), may hold values from -6 to 6
- grad_out: bfloat16 [2, 12288, 3072], P('dp', ('tile', 'head')), may hold values from -6 to 6
- neighbours: int32 [2, 32, 4], P('dp'), may hold values from -1 to 31, as said below
Outputs:
- attended: bfloat16 [2, 12288, 3072], P('dp', ('tile', 'head'))
- grad_queries: bfloat16 [2, 12288, 3072], P('dp', ('tile', 'head'))
- grad_keys: bfloat16 [2, 12288, 3072], P('dp', ('tile', 'head'))
- grad_values: bfloat16 [2, 12288, 3072], P('dp', ('tile', 'head'))
Inputs may be any that keep to these rules, and one draw needn't show every extreme that they name: `neighbours`: entry 0 of each list is the query tile itself. The other entries are distinct tiles other than it, each in the same block of 4 tiles as the query tile or in a block right beside it, followed by -1 for unused slots; each list has between 2 and 4 used entries.
All inputs are finite; a program needn't handle non-finite values.
Results may differ from a plain program's by a relative error of at most 0.029.
Values may be sent and summed in bfloat16 or wider, within the bound.
A program may use at most 128 MiB of HBM per device.

v0:
```python
import jax
import jax.numpy as jnp
from jax import lax
from jax.sharding import PartitionSpec as P

HD = 128
TILE = 384
NBR = 4


def with_halo(cells, sides, width):
    for axis, dim in sides:
        count = lax.axis_size(axis)
        ends = count - 1
        head = lax.slice_in_dim(cells, 0, width, axis=dim)
        tail = lax.slice_in_dim(cells, cells.shape[dim] - width, cells.shape[dim], axis=dim)
        cells = jnp.concatenate(
            [
                lax.ppermute(tail, axis, [(i, (i + 1) % count) for i in range(ends)]),
                cells,
                lax.ppermute(head, axis, [((i + 1) % count, i) for i in range(ends)]),
            ],
            axis=dim,
        )
    return cells


def from_behind(block, axis, distance):
    devices = range(lax.axis_size(axis))
    route = [(i - distance, i) for i in devices if i - distance in devices]
    return lax.ppermute(block, axis, route)


def head_major(block):
    count = block.shape[1]
    return block[0].reshape(count, block.shape[2] // HD, HD).transpose(1, 0, 2)


def token_major(block):
    return block.transpose(1, 0, 2).reshape(1, block.shape[1], block.shape[0] * block.shape[2])


def tile_scores(q_now, k_now, mask_row):
    scores = jnp.einsum("hqd,hkd->hqk", q_now, k_now, preferred_element_type=jnp.float32) * HD ** (
        -0.5
    )
    return jnp.where(mask_row[None, None, :], scores, -1e30)


def body(queries, keys, values, grad_out, neighbours):
    q_all, k_all, v_all, g_all = (
        lax.all_to_all(queries, "head", split_axis=2, concat_axis=1, tiled=True),
        lax.all_to_all(keys, "head", split_axis=2, concat_axis=1, tiled=True),
        lax.all_to_all(values, "head", split_axis=2, concat_axis=1, tiled=True),
        lax.all_to_all(grad_out, "head", split_axis=2, concat_axis=1, tiled=True),
    )
    rows = q_all.shape[1]
    tiles = rows // TILE
    q_head = head_major(q_all)
    g_head = head_major(g_all)
    paired = jnp.stack([head_major(k_all), head_major(v_all)])
    per_dev = q_head.shape[0]
    extended = with_halo(paired, (("tile", 2),), rows)
    first = lax.axis_index("tile") * tiles
    mine = lax.dynamic_slice_in_dim(neighbours[0], first, tiles, 0)
    usable = mine >= 0
    local = jnp.where(usable, mine - first + tiles, tiles)
    slot_mask = jnp.repeat(usable, TILE, axis=1)

    def pick(index):
        starts = local[index] * TILE
        pieces = [lax.dynamic_slice_in_dim(extended, starts[slot], TILE, 2) for slot in range(NBR)]
        return jnp.concatenate(pieces, axis=2)

    def forward_step(out_buf, index):
        chosen = pick(index)
        q_now = lax.dynamic_slice_in_dim(q_head, index * TILE, TILE, 1)
        scores = tile_scores(q_now, chosen[0], slot_mask[index])
        peak = jnp.max(scores, axis=2, keepdims=True)
        expo = jnp.exp(scores - peak)
        total = jnp.sum(expo, axis=2, keepdims=True)
        probs = (expo / total).astype(jnp.bfloat16)
        result = jnp.einsum(
            "hqk,hkd->hqd", probs, chosen[1], preferred_element_type=jnp.float32
        ).astype(jnp.bfloat16)
        out_buf = lax.dynamic_update_slice_in_dim(out_buf, result, index * TILE, 1)
        return (out_buf, (peak, total))

    out_start = jnp.zeros((per_dev, rows, HD), jnp.bfloat16)
    indices = jnp.arange(tiles, dtype=jnp.int32)
    out_head, (peaks, totals) = lax.scan(forward_step, out_start, indices)
    out_rows = token_major(out_head)

    def backward_step(carry, index):
        dq_buf, accum = carry
        chosen = pick(index)
        k_now = chosen[0]
        v_now = chosen[1]
        q_now = lax.dynamic_slice_in_dim(q_head, index * TILE, TILE, 1)
        g_now = lax.dynamic_slice_in_dim(g_head, index * TILE, TILE, 1)
        result = lax.dynamic_slice_in_dim(out_head, index * TILE, TILE, 1)
        scores = tile_scores(q_now, k_now, slot_mask[index])
        weight = jnp.exp(scores - peaks[index]) / totals[index]
        probs = weight.astype(jnp.bfloat16)
        delta = jnp.sum(g_now.astype(jnp.float32) * result.astype(jnp.float32), axis=-1)
        dprobs = jnp.einsum("hqd,hkd->hqk", g_now, v_now, preferred_element_type=jnp.float32)
        dscores = (weight * (dprobs - delta[:, :, None]) * HD ** (-0.5)).astype(jnp.bfloat16)
        dq_now = jnp.einsum(
            "hqk,hkd->hqd", dscores, k_now, preferred_element_type=jnp.float32
        ).astype(jnp.bfloat16)
        dk_part = jnp.einsum("hqk,hqd->hkd", dscores, q_now, preferred_element_type=jnp.float32)
        dv_part = jnp.einsum("hqk,hqd->hkd", probs, g_now, preferred_element_type=jnp.float32)
        both = jnp.stack([dk_part, dv_part])
        starts = local[index] * TILE
        for slot in range(NBR):
            current = lax.dynamic_slice_in_dim(accum, starts[slot], TILE, 2)
            addend = both[:, :, slot * TILE : (slot + 1) * TILE]
            accum = lax.dynamic_update_slice_in_dim(accum, current + addend, starts[slot], 2)
        dq_buf = lax.dynamic_update_slice_in_dim(dq_buf, dq_now, index * TILE, 1)
        return ((dq_buf, accum), None)

    accum_start = jnp.zeros((2, per_dev, 3 * rows, HD), jnp.float32)
    (dq_head, accum), unused = lax.scan(backward_step, (out_start, accum_start), indices)
    lower_rim = accum[:, :, :rows].astype(jnp.bfloat16)
    own_part = accum[:, :, rows : 2 * rows]
    upper_rim = accum[:, :, 2 * rows :].astype(jnp.bfloat16)
    from_lower = from_behind(upper_rim, "tile", 1)
    from_upper = from_behind(lower_rim, "tile", -1)
    grads = (own_part + from_lower.astype(jnp.float32) + from_upper.astype(jnp.float32)).astype(
        jnp.bfloat16
    )
    dq_rows = token_major(dq_head)
    dk_rows = token_major(grads[0])
    dv_rows = token_major(grads[1])
    out_home, dq_home, dk_home, dv_home = (
        lax.all_to_all(out_rows, "head", split_axis=1, concat_axis=2, tiled=True),
        lax.all_to_all(dq_rows, "head", split_axis=1, concat_axis=2, tiled=True),
        lax.all_to_all(dk_rows, "head", split_axis=1, concat_axis=2, tiled=True),
        lax.all_to_all(dv_rows, "head", split_axis=1, concat_axis=2, tiled=True),
    )
    return (out_home, dq_home, dk_home, dv_home)


def solution(mesh):
    placed = (
        P("dp", ("tile", "head"), None),
        P("dp", ("tile", "head"), None),
        P("dp", ("tile", "head"), None),
        P("dp", ("tile", "head"), None),
        P("dp", None, None),
    )
    return jax.shard_map(
        body,
        mesh=mesh,
        in_specs=placed,
        out_specs=(
            P("dp", ("tile", "head"), None),
            P("dp", ("tile", "head"), None),
            P("dp", ("tile", "head"), None),
            P("dp", ("tile", "head"), None),
        ),
        check_vma=False,
    )
```

profile of v0, /device:TPU:6, one launch (start us, length us, event | category | flops | bytes accessed | tf_op | source)
XLA Modules:
  0.0 836.6 jit_solution(16073283266449677286)
XLA Ops:
  0.6 7.6 copy.95
  8.7 18.2 %reduce.6 = bf16[3072,192]{1,0:T(8,128)(2,1)} reduce(bf16[3072,1,192]{2,1,0:T(2,128)(2,1)S(1)} %bitcast.202, bf16[]{:T(256)} %broadcast.57), dimensions={1}, to_apply=%bitcast.134.reduce_sub_computation | reduce | bytes 2359298
  31.5 5.9 all-to-all-start.1
  37.5 7.5 copy.98
  45.0 18.2 %reduce.5 = bf16[3072,192]{1,0:T(8,128)(2,1)} reduce(bf16[3072,1,192]{2,1,0:T(2,128)(2,1)S(1)} %bitcast.203, bf16[]{:T(256)} %broadcast.57), dimensions={1}, to_apply=%bitcast.132.reduce_sub_computation | reduce | bytes 2359298
  67.8 6.0 all-to-all-start.2
  78.8 6.0 copy.96
  95.5 6.0 copy.99
  118.4 7.6 copy.91
  126.0 18.3 %reduce.4 = bf16[3072,192]{1,0:T(8,128)(2,1)} reduce(bf16[3072,1,192]{2,1,0:T(2,128)(2,1)S(1)} %bitcast.204, bf16[]{:T(256)} %broadcast.57), dimensions={1}, to_apply=%bitcast.130.reduce_sub_computation | reduce | bytes 2359298
  154.6 7.5 copy.106
  162.1 18.3 %reduce.8 = bf16[3072,192]{1,0:T(8,128)(2,1)} reduce(bf16[3072,1,192]{2,1,0:T(2,128)(2,1)S(1)} %bitcast.205, bf16[]{:T(256)} %broadcast.57), dimensions={1}, to_apply=%bitcast.138.reduce_sub_computation | reduce | bytes 2359298
  185.0 42.6 %all-to-all-done = bf16[8,2,36864]{2,1,0:T(2,128)(2,1)} async-done(((bf16[8,2,36864]{2,1,0:T(2,128)(2,1)}), bf16[8,2,36864]{2,1,0:T(2,128)(2,1)}, u32[]{:S(2)}, u32[]{:S(2)}) %all-to-all-start) | async-done | bytes 1179680 | tf_op jit(solution)/shard_map/all_to_all | solution.py:52
  227.6 8.0 all-to-all-start.4
  241.2 6.0 copy.92
  258.4 6.0 copy.107
  277.9 10.3 %copy.102 = bf16[2,3,4608,128]{3,2,1,0:T(8,128)(2,1)} copy(bf16[2,3,4608,128]{2,3,1,0:T(8,128)(2,1)} %pad_maximum_fusion.3) | data formatting | bytes 14155776 | tf_op jit(solution)/shard_map/while | solution.py:91
  288.4 80.2 %while.26 = (s32[]{:T(128)}, bf16[3,1536,128]{2,1,0:T(8,128)(2,1)S(1)}, f32[4,3,384,1]{2,1,3,0:T(4,128)S(1)}, f32[4,3,384,1]{2,1,3,0:T(4,128)S(1)}, s32[4]{0:T(1...) while((s32[]{:T(128)}, ...), condition=%wide.region_3.4_spmd, body=%wide.region_0.3_spmd.sunk | while | flops 936785664 | bytes 33679836 | solution.py:91
  369.8 6.0 broadcast_in_dim.47
  375.8 232.9 %while.27 = (s32[]{:T(128)}, bf16[3,1536,128]{1,2,0:T(8,128)(2,1)}, f32[2,3,4608,128]{3,2,1,0:T(8,128)}, s32[4]{0:T(128)S(1)}, pred[4,1536]{1,0:T(4,128)(4,1)S(1...) while((s32[]{:T(128)}, bf16[3,1536,128]{1,2,0:T(8,128)(2,1)}, ...), condition=%wide.region_6.7_spmd, body=%wide.region_4.6_spmd.sunk | while | flops 2293382144 | bytes 101497024 | solution.py:123
  404.8 6.1 dynamic_update_slice.39
  412.5 6.1 dynamic_update_slice.40
  420.3 6.1 dynamic_update_slice.41
  428.0 6.2 dynamic_update_slice.42
  463.1 6.1 dynamic_update_slice.39
  470.8 6.1 dynamic_update_slice.40
  478.4 6.1 dynamic_update_slice.41
  486.2 6.2 dynamic_update_slice.42
  521.3 6.1 dynamic_update_slice.39
  529.0 6.1 dynamic_update_slice.40
  536.7 6.1 dynamic_update_slice.41
  544.4 6.2 dynamic_update_slice.42
  579.4 6.1 dynamic_update_slice.39
  587.2 6.1 dynamic_update_slice.40
  594.8 6.1 dynamic_update_slice.41
  602.5 6.2 dynamic_update_slice.42
  608.7 15.2 %copy.115 = f32[2,3,4608,128]{2,3,1,0:T(8,128)} copy(f32[2,3,4608,128]{3,2,1,0:T(8,128)} %get-tuple-element.120) | data formatting | bytes 28311552 | tf_op jit(solution)/shard_map/while | solution.py:123
  623.9 8.6 %convert.4 = bf16[2,3,4608,128]{2,3,1,0:T(8,128)(2,1)} convert(f32[2,3,4608,128]{2,3,1,0:T(8,128)} %copy.115) | non-fusion elementwise | flops 3538944 | bytes 21233664 | tf_op jit(solution)/shard_map/convert.1
  650.3 9.0 %reduce.7 = bf16[1536,384]{1,0:T(8,128)(2,1)S(1)} reduce(bf16[1536,1,384]{2,1,0:T(2,128)(2,1)S(1)} %bitcast.215, bf16[]{:T(256)} %broadcast.57), dimensions={1}, to_apply=%bitcast.136.reduce_sub_computation | reduce | bytes 2359298
  666.2 6.3 copy.113
  672.5 10.0 %reduce.9 = bf16[1536,384]{1,0:T(8,128)(2,1)} reduce(bf16[1536,1,384]{2,1,0:T(2,128)(2,1)S(1)} %bitcast.216, bf16[]{:T(256)} %broadcast.57), dimensions={1}, to_apply=%bitcast.140.reduce_sub_computation | reduce | bytes 2359298
  684.7 68.9 %all-to-all-done.3 = bf16[8,2,36864]{2,1,0:T(2,128)(2,1)S(1)} async-done(((bf16[8,2,36864]{2,1,0:T(2,128)(2,1)}), bf16[8,2,36864]{2,1,0:T(2,128)(2,1)S(1)}, u32[]{:S(2)}, u32[]{:S(2)}) %all-to-all-start.3) | async-done | bytes 1179680 | tf_op jit(solution)/shard_map/all_to_all | solution.py:136
  753.6 7.5 all-to-all-start.5
  767.3 6.3 copy.117
  773.6 10.0 %reduce.10 = bf16[1536,384]{1,0:T(8,128)(2,1)} reduce(bf16[1536,1,384]{2,1,0:T(2,128)(2,1)S(1)} %bitcast.217, bf16[]{:T(256)} %broadcast.57), dimensions={1}, to_apply=%bitcast.142.reduce_sub_computation | reduce | bytes 2359298
  785.9 6.0 all-to-all-start.6
  791.9 6.3 copy.119
  798.2 10.0 %reduce.11 = bf16[1536,384]{1,0:T(8,128)(2,1)} reduce(bf16[1536,1,384]{2,1,0:T(2,128)(2,1)S(1)} %bitcast.214, bf16[]{:T(256)} %broadcast.57), dimensions={1}, to_apply=%bitcast.144.reduce_sub_computation | reduce | bytes 2359298
  (265 shorter events, 284.9 us)
Async XLA Ops:
  31.5 36.3 %all-to-all-start.1 = ((bf16[8,2,36864]{2,1,0:T(2,128)(2,1)}), bf16[8,2,36864]{2,1,0:T(2,128)(2,1)}, u32[]{:S(2)}, u32[]{:S(2)}) async-start(bf16[8,2,36864]{2,1,0:T(2,128)(2,1)} %reshape.74), calls=%async_computation.1 | async-start | bytes 2359296 | tf_op jit(solution)/shard_map/all_to_all | solution.py:53
  67.8 22.6 %all-to-all-start.2 = ((bf16[8,2,36864]{2,1,0:T(2,128)(2,1)}), bf16[8,2,36864]{2,1,0:T(2,128)(2,1)}, u32[]{:S(2)}, u32[]{:S(2)}) async-start(bf16[8,2,36864]{2,1,0:T(2,128)(2,1)} %reshape.72), calls=%async_computation.2 | async-start | bytes 2359296 | tf_op jit(solution)/shard_map/all_to_all | solution.py:54
  103.1 5.3 copy-start.2
  108.4 1.8 copy-start.4
  110.2 162.0 %collective-permute-start.1 = (bf16[2,3,1536,128]{2,3,1,0:T(8,128)(2,1)}, bf16[2,3,1536,128]{2,3,1,0:T(8,128)(2,1)}, u32[]{:S(2)}, u32[]{:S(2)}) collective-permute-start(bf16[2,3,1536,128]{2,3,1,0:T(8,128)(2,1)} %pad_maximum_fusion.4), channel_id=1, source_target_pairs={{16,0},{32,16},{48,32},{64,48},{80,64},{96,80},{112,96},{17,1},{33... | collective-permute-start | bytes 7077896 | tf_op jit(solution)/shard_map/ppermute | solution.py:21
  113.5 158.7 %collective-permute-start = (bf16[2,3,1536,128]{2,3,1,0:T(8,128)(2,1)}, bf16[2,3,1536,128]{2,3,1,0:T(8,128)(2,1)}, u32[]{:S(2)}, u32[]{:S(2)}) collective-permute-start(bf16[2,3,1536,128]{2,3,1,0:T(8,128)(2,1)} %pad_maximum_fusion.4), channel_id=1, source_target_pairs={{0,16},{16,32},{32,48},{48,64},{64,80},{80,96},{96,112},{1,17},{17... | collective-permute-start | bytes 7077896 | tf_op jit(solution)/shard_map/ppermute | solution.py:19
  148.9 78.7 %all-to-all-start = ((bf16[8,2,36864]{2,1,0:T(2,128)(2,1)}), bf16[8,2,36864]{2,1,0:T(2,128)(2,1)}, u32[]{:S(2)}, u32[]{:S(2)}) async-start(bf16[8,2,36864]{2,1,0:T(2,128)(2,1)} %reshape.70), calls=%async_computation | async-start | bytes 2359296 | tf_op jit(solution)/shard_map/all_to_all | solution.py:52
  180.4 55.3 %copy-start.12 = (s32[1,32,4]{1,2,0:T(4,128)S(1)}, s32[1,32,4]{1,2,0:T(4,128)}, u32[]{:S(2)}) copy-start(s32[1,32,4]{1,2,0:T(4,128)} %param.13) | copy-start | bytes 1540
  227.6 25.7 %all-to-all-start.4 = ((bf16[8,2,36864]{2,1,0:T(2,128)(2,1)}), bf16[8,2,36864]{2,1,0:T(2,128)(2,1)}, u32[]{:S(2)}, u32[]{:S(2)}) async-start(bf16[8,2,36864]{2,1,0:T(2,128)(2,1)} %reshape.78), calls=%async_computation.4 | async-start | bytes 2359296 | tf_op jit(solution)/shard_map/all_to_all | solution.py:55
  266.0 6.2 copy-start.3
  266.0 6.2 copy-start.5
  277.9 10.5 %copy-start.6 = (f32[4,3,384,1]{2,1,3,0:T(4,128)S(1)}, f32[4,3,384,1]{2,1,3,0:T(4,128)}, u32[]{:S(2)}) copy-start(f32[4,3,384,1]{2,1,3,0:T(4,128)} %custom-call.1) | copy-start | bytes 55300
  277.9 10.5 %copy-start.9 = (f32[4,3,384,1]{2,1,3,0:T(4,128)S(1)}, f32[4,3,384,1]{2,1,3,0:T(4,128)}, u32[]{:S(2)}) copy-start(f32[4,3,384,1]{2,1,3,0:T(4,128)} %custom-call) | copy-start | bytes 55300
  376.0 11.4 %copy-start.7 = (f32[4,3,384,1]{2,1,3,0:T(4,128)}, f32[4,3,384,1]{2,1,3,0:T(4,128)S(1)}, u32[]{:S(2)}) copy-start(f32[4,3,384,1]{2,1,3,0:T(4,128)S(1)} %get-tuple-element.535) | copy-start | bytes 55300 | tf_op jit(solution)/shard_map/while
  376.0 11.4 %copy-start.10 = (f32[4,3,384,1]{2,1,3,0:T(4,128)}, f32[4,3,384,1]{2,1,3,0:T(4,128)S(1)}, u32[]{:S(2)}) copy-start(f32[4,3,384,1]{2,1,3,0:T(4,128)S(1)} %get-tuple-element.534) | copy-start | bytes 55300 | tf_op jit(solution)/shard_map/while
  376.0 15.3 %copy-start = (bf16[3,1536,128]{2,1,0:T(8,128)(2,1)}, bf16[3,1536,128]{2,1,0:T(8,128)(2,1)S(1)}, u32[]{:S(2)}) copy-start(bf16[3,1536,128]{2,1,0:T(8,128)(2,1)S(1)} %get-tuple-element.537) | copy-start | bytes 3538948 | tf_op jit(solution)/shard_map/while
  428.0 6.2 copy-start.1
  428.0 6.2 copy-start.8
  428.0 6.2 copy-start.11
  434.2 11.4 %copy-start.7 = (f32[4,3,384,1]{2,1,3,0:T(4,128)}, f32[4,3,384,1]{2,1,3,0:T(4,128)S(1)}, u32[]{:S(2)}) copy-start(f32[4,3,384,1]{2,1,3,0:T(4,128)S(1)} %get-tuple-element.535) | copy-start | bytes 55300 | tf_op jit(solution)/shard_map/while
  434.2 11.4 %copy-start.10 = (f32[4,3,384,1]{2,1,3,0:T(4,128)}, f32[4,3,384,1]{2,1,3,0:T(4,128)S(1)}, u32[]{:S(2)}) copy-start(f32[4,3,384,1]{2,1,3,0:T(4,128)S(1)} %get-tuple-element.534) | copy-start | bytes 55300 | tf_op jit(solution)/shard_map/while
  434.2 15.3 %copy-start = (bf16[3,1536,128]{2,1,0:T(8,128)(2,1)}, bf16[3,1536,128]{2,1,0:T(8,128)(2,1)S(1)}, u32[]{:S(2)}) copy-start(bf16[3,1536,128]{2,1,0:T(8,128)(2,1)S(1)} %get-tuple-element.537) | copy-start | bytes 3538948 | tf_op jit(solution)/shard_map/while
  486.1 6.2 copy-start.1
  486.1 6.2 copy-start.8
  486.1 6.2 copy-start.11
  492.4 11.4 %copy-start.7 = (f32[4,3,384,1]{2,1,3,0:T(4,128)}, f32[4,3,384,1]{2,1,3,0:T(4,128)S(1)}, u32[]{:S(2)}) copy-start(f32[4,3,384,1]{2,1,3,0:T(4,128)S(1)} %get-tuple-element.535) | copy-start | bytes 55300 | tf_op jit(solution)/shard_map/while
  492.4 11.4 %copy-start.10 = (f32[4,3,384,1]{2,1,3,0:T(4,128)}, f32[4,3,384,1]{2,1,3,0:T(4,128)S(1)}, u32[]{:S(2)}) copy-start(f32[4,3,384,1]{2,1,3,0:T(4,128)S(1)} %get-tuple-element.534) | copy-start | bytes 55300 | tf_op jit(solution)/shard_map/while
  492.4 15.3 %copy-start = (bf16[3,1536,128]{2,1,0:T(8,128)(2,1)}, bf16[3,1536,128]{2,1,0:T(8,128)(2,1)S(1)}, u32[]{:S(2)}) copy-start(bf16[3,1536,128]{2,1,0:T(8,128)(2,1)S(1)} %get-tuple-element.537) | copy-start | bytes 3538948 | tf_op jit(solution)/shard_map/while
  544.3 6.2 copy-start.1
  544.4 6.2 copy-start.8
  544.4 6.2 copy-start.11
  550.6 11.4 %copy-start.7 = (f32[4,3,384,1]{2,1,3,0:T(4,128)}, f32[4,3,384,1]{2,1,3,0:T(4,128)S(1)}, u32[]{:S(2)}) copy-start(f32[4,3,384,1]{2,1,3,0:T(4,128)S(1)} %get-tuple-element.535) | copy-start | bytes 55300 | tf_op jit(solution)/shard_map/while
  550.6 11.4 %copy-start.10 = (f32[4,3,384,1]{2,1,3,0:T(4,128)}, f32[4,3,384,1]{2,1,3,0:T(4,128)S(1)}, u32[]{:S(2)}) copy-start(f32[4,3,384,1]{2,1,3,0:T(4,128)S(1)} %get-tuple-element.534) | copy-start | bytes 55300 | tf_op jit(solution)/shard_map/while
  550.6 15.3 %copy-start = (bf16[3,1536,128]{2,1,0:T(8,128)(2,1)}, bf16[3,1536,128]{2,1,0:T(8,128)(2,1)S(1)}, u32[]{:S(2)}) copy-start(bf16[3,1536,128]{2,1,0:T(8,128)(2,1)S(1)} %get-tuple-element.537) | copy-start | bytes 3538948 | tf_op jit(solution)/shard_map/while
  602.5 6.2 copy-start.1
  602.5 6.2 copy-start.8
  602.5 6.2 copy-start.11
  637.4 123.7 %collective-permute-start.2 = (bf16[2,3,1536,128]{2,3,1,0:T(8,128)(2,1)}, bf16[2,3,1536,128]{2,3,1,0:T(8,128)(2,1)}, u32[]{:S(2)}, u32[]{:S(2)}) collective-permute-start(bf16[2,3,1536,128]{2,3,1,0:T(8,128)(2,1)} %get-tuple-element.269), channel_id=1, source_target_pairs={{0,16},{16,32},{32,48},{48,64},{64,80},{80,96},{96,112},{1,17},{17... | collective-permute-start | bytes 7077896 | tf_op jit(solution)/shard_map/ppermute | solution.py:31
  642.4 118.6 %collective-permute-start.3 = (bf16[2,3,1536,128]{2,3,1,0:T(8,128)(2,1)}, bf16[2,3,1536,128]{2,3,1,0:T(8,128)(2,1)}, u32[]{:S(2)}, u32[]{:S(2)}) collective-permute-start(bf16[2,3,1536,128]{2,3,1,0:T(8,128)(2,1)} %get-tuple-element.270), channel_id=1, source_target_pairs={{16,0},{32,16},{48,32},{64,48},{80,64},{96,80},{112,96},{17,1},{33... | collective-permute-start | bytes 7077896 | tf_op jit(solution)/shard_map/ppermute | solution.py:31
  660.5 93.1 %all-to-all-start.3 = ((bf16[8,2,36864]{2,1,0:T(2,128)(2,1)}), bf16[8,2,36864]{2,1,0:T(2,128)(2,1)S(1)}, u32[]{:S(2)}, u32[]{:S(2)}) async-start(bf16[8,2,36864]{2,1,0:T(2,128)(2,1)} %reshape.76), calls=%async_computation.3 | async-start | bytes 2359296 | tf_op jit(solution)/shard_map/all_to_all | solution.py:136
  753.6 32.3 %all-to-all-start.5 = ((bf16[8,2,36864]{2,1,0:T(2,128)(2,1)}), bf16[8,2,36864]{2,1,0:T(2,128)(2,1)}, u32[]{:S(2)}, u32[]{:S(2)}) async-start(bf16[8,2,36864]{2,1,0:T(2,128)(2,1)} %reshape.80), calls=%async_computation.5 | async-start | bytes 2359296 | tf_op jit(solution)/shard_map/all_to_all | solution.py:137
  785.9 24.6 %all-to-all-start.6 = ((bf16[8,2,36864]{2,1,0:T(2,128)(2,1)}), bf16[8,2,36864]{2,1,0:T(2,128)(2,1)}, u32[]{:S(2)}, u32[]{:S(2)}) async-start(bf16[8,2,36864]{2,1,0:T(2,128)(2,1)} %reshape.82), calls=%async_computation.6 | async-start | bytes 2359296 | tf_op jit(solution)/shard_map/all_to_all | solution.py:138
  810.5 19.9 %all-to-all-start.7 = ((bf16[8,2,36864]{2,1,0:T(2,128)(2,1)}), bf16[8,2,36864]{2,1,0:T(2,128)(2,1)}, u32[]{:S(2)}, u32[]{:S(2)}) async-start(bf16[8,2,36864]{2,1,0:T(2,128)(2,1)} %reshape.84), calls=%async_computation.7 | async-start | bytes 2359296 | tf_op jit(solution)/shard_map/all_to_all | solution.py:139
where the time goes:
time: 852 us; the launch traced here: 837 us
  local copies, waits for them, and re-layouts  346 us (41%)
  other arithmetic  167 us (20%)
  waiting for transfers between devices  111 us (13%)
  loops' own time  81.9 us (10%)
  starting transfers between devices  67.6 us (8%)
  matrix products  61.3 us (7%)
    unnamed x8, other arithmetic  112 us
    unnamed x45, local copies, waits for them, and re-layouts  98.1 us
    dynamic_update_slice x16, local copies, waits for them, and re-layouts, backward_step(): lax.dynamic_update_slice_in_dim(accum, current + addend, starts[slot], 2)  97.9 us
    all_to_all x1, waiting for transfers between devices, body(): lax.all_to_all(out_rows, 'head', split_axis=1, concat_axis=2, tiled=True)  68.9 us
    all_to_all x1, waiting for transfers between devices, body(): lax.all_to_all(queries, 'head', split_axis=2, concat_axis=1, tiled=True)  42.6 us
    another operation x1, loops' own time, body(): out_head, (peaks, totals) = lax.scan(forward_step, out_start, indices)  41.1 us
    another operation x1, loops' own time, body(): lax.scan(backward_step, (out_start, accum_start), indices)  40.7 us
    add x16, other arithmetic, backward_step(): current + addend  25.5 us
  transfers between devices with their start and end apart: 12, of which 2 were waited for; matrix products, arithmetic and copies ran while one was open for 28% of the time, Pallas kernels for 0%

commit v1 on v0

v1 whole, which is shorter than its diff:
```python
import functools
import math

import jax
import jax.numpy as jnp
from jax import lax
from jax.experimental import pallas as pl
from jax.experimental.pallas import tpu as pltpu
from jax.sharding import PartitionSpec as P

HD = 128
TILE = 384
NBR = 4
TILES = 4
GROUP = 3
CHUNK = 64
MESH = pl.DeviceIdType.MESH
F32 = jnp.float32
BF16 = jnp.bfloat16
NT = (((1,), (1,)), ((), ()))
NN = (((1,), (0,)), ((), ()))
TN = (((0,), (0,)), ((), ()))


def dot(a, b, dims):
    return lax.dot_general(a, b, dims, preferred_element_type=F32)


def kernel(slabs, groups, *refs):
    args, places_ref, shares_ref, outs = refs[:4], refs[4], refs[5], refs[6:10]
    it = iter(refs[10:])

    def take(n):
        return [next(it) for _ in range(n)]

    qs, gs, ks, vs = take(GROUP), take(GROUP), take(GROUP), take(GROUP)
    os, dqs, dks, dvs = take(GROUP), take(GROUP), take(GROUP), take(GROUP)
    own_k, own_v = take(GROUP), take(GROUP)
    rim_out = [take(4) for _ in range(GROUP)]
    rim_in = [take(4) for _ in range(GROUP)]
    s_ref, e_ref, d_ref, dkc, dvc = take(5)
    (send_in, recv_in, halo_send, halo_recv, rim_send, rim_recv, send_out, recv_out) = take(8)

    tile = lax.axis_index("tile")
    group = lax.axis_index("head")
    core = lax.axis_index("dp")
    z = tile // 2
    side = tile % 2
    slab = 2 * z + core
    rows = TILES * TILE
    block = rows // groups
    has_self = core == side
    column = (2 * z + core, side)

    below, above = slab - 1, slab + 1
    low_id = (2 * (lax.max(below, 0) // 2) + side, group, lax.max(below, 0) % 2)
    high_id = (2 * (lax.min(above, slabs - 1) // 2) + side, group, lax.min(above, slabs - 1) % 2)
    has_low, has_high = slab > 0, slab < slabs - 1

    barrier = pltpu.get_barrier_semaphore()

    def greet(i, _):
        g = (group + i) % groups

        @pl.when(jnp.logical_or(jnp.logical_not(has_self), g != group))
        def _():
            pl.semaphore_signal(barrier, inc=1, device_id=(column[0], g, column[1]), device_id_type=MESH)

        return 0

    lax.fori_loop(0, groups, greet, 0)

    @pl.when(has_low)
    def _():
        pl.semaphore_signal(barrier, inc=1, device_id=low_id, device_id_type=MESH)

    @pl.when(has_high)
    def _():
        pl.semaphore_signal(barrier, inc=1, device_id=high_id, device_id_type=MESH)

    count = groups - has_self.astype(jnp.int32) + has_low.astype(jnp.int32) + has_high.astype(jnp.int32)
    pl.semaphore_wait(barrier, count)

    def spread(a, j, dst, offset):
        def step(i, _):
            g = (group + i) % groups
            src = args[a].at[0, :, pl.ds(pl.multiple_of((g * GROUP + j) * HD, HD), HD)]
            to = dst.at[offset + group * block // TILE, pl.ds(pl.multiple_of(group * block % TILE, block), block), :]
            here = jnp.logical_and(has_self, g == group)

            @pl.when(here)
            def _():
                pltpu.make_async_copy(src, to, recv_in.at[a, j]).start()

            @pl.when(jnp.logical_not(here))
            def _():
                pltpu.make_async_remote_copy(
                    src_ref=src, dst_ref=to, send_sem=send_in.at[a], recv_sem=recv_in.at[a, j],
                    device_id=(column[0], g, column[1]), device_id_type=MESH,
                ).start()

            return 0

        lax.fori_loop(0, groups, step, 0)

    def arrived(a, j, dst, offset):
        view = dst.at[pl.ds(offset, TILES)]
        pltpu.make_async_copy(view, view, recv_in.at[a, j]).wait()

    def home(a, j, src):
        def step(i, _):
            g = (group + i) % groups
            piece = src.at[g * block // TILE, pl.ds(pl.multiple_of(g * block % TILE, block), block), :]
            to = outs[a].at[0, :, pl.ds(pl.multiple_of((group * GROUP + j) * HD, HD), HD)]
            here = jnp.logical_and(has_self, g == group)

            @pl.when(here)
            def _():
                pltpu.make_async_copy(piece, to, recv_out.at[a]).start()

            @pl.when(jnp.logical_not(here))
            def _():
                pltpu.make_async_remote_copy(
                    src_ref=piece, dst_ref=to, send_sem=send_out.at[a], recv_sem=recv_out.at[a],
                    device_id=(column[0], g, column[1]), device_id_type=MESH,
                ).start()

            return 0

        lax.fori_loop(0, groups, step, 0)

    def halo(j, n, direction):
        src = (ks, vs)[n][j]
        return pltpu.make_async_remote_copy(
            src_ref=src.at[pl.ds(TILES, TILES)],
            dst_ref=src.at[pl.ds(0 if direction else 2 * TILES, TILES)],
            send_sem=halo_send.at[j, n, direction], recv_sem=halo_recv.at[j, n, direction],
            device_id=high_id if direction else low_id, device_id_type=MESH,
        )

    def rim(j, n, direction):
        return pltpu.make_async_remote_copy(
            src_ref=rim_out[j][2 * direction + n], dst_ref=rim_in[j][2 * (1 - direction) + n],
            send_sem=rim_send.at[j, n, direction], recv_sem=rim_recv.at[j, n, direction],
            device_id=high_id if direction else low_id, device_id_type=MESH,
        )

    def both(make, j, act):
        for direction in range(2):
            there = (has_low, has_high)[direction]
            source = (has_high, has_low)[direction]
            if act == "start":
                @pl.when(there)
                def _():
                    for n in range(2):
                        make(j, n, direction).start()
            elif act == "recv":
                @pl.when(source)
                def _():
                    for n in range(2):
                        make(j, n, direction).wait_recv()
            else:
                @pl.when(there)
                def _():
                    for n in range(2):
                        make(j, n, direction).wait_send()

    scale = HD ** -0.5
    to_two = scale * math.log2(math.e)

    def attend(j, a):
        starts, hides = [], []
        for s in range(NBR):
            starts.append(places_ref[a * NBR + s])
            hides.append(shares_ref[a * NBR + s])
        q = qs[j][a]
        peak = jnp.full((1, TILE), -1e30, F32)
        for s in range(NBR):
            scores = dot(ks[j][starts[s]], q, NT)
            s_ref[s * TILE:(s + 1) * TILE, :] = scores
            peak = jnp.maximum(peak, jnp.max(scores, axis=0, keepdims=True) - hides[s])
        total = jnp.zeros((1, TILE), F32)
        for s in range(NBR):
            floor = peak + hides[s]
            for c in range(0, TILE, CHUNK):
                part = slice(s * TILE + c, s * TILE + c + CHUNK)
                expo = jnp.exp2((s_ref[part, :] - floor) * to_two)
                total = total + jnp.sum(expo, axis=0, keepdims=True)
                e_ref[part, :] = expo.astype(BF16)
        inverse = 1.0 / total
        g_cols = (gs[j][a].astype(F32).T * inverse).astype(BF16)
        attended = jnp.zeros((HD, TILE), F32)
        delta = jnp.zeros((1, TILE), F32)
        for s in range(NBR):
            v = vs[j][starts[s]]
            span = slice(s * TILE, (s + 1) * TILE)
            s_ref[span, :] = dot(v, g_cols, NN)
            dvc[a * NBR + s] = dot(e_ref[span, :], g_cols, NT)
            attended = attended + dot(v, e_ref[span, :], TN)
            for c in range(0, TILE, CHUNK):
                part = slice(s * TILE + c, s * TILE + c + CHUNK)
                delta = delta + jnp.sum(e_ref[part, :].astype(F32) * s_ref[part, :], axis=0, keepdims=True)
        os[j][a] = (attended * inverse).T.astype(BF16)
        delta = delta * inverse
        grad_q = jnp.zeros((HD, TILE), F32)
        for s in range(NBR):
            for c in range(0, TILE, CHUNK):
                part = slice(s * TILE + c, s * TILE + c + CHUNK)
                d_ref[part, :] = (e_ref[part, :].astype(F32) * (s_ref[part, :] - delta)).astype(BF16)
            span = slice(s * TILE, (s + 1) * TILE)
            dkc[a * NBR + s] = dot(d_ref[span, :], q, NN) * scale
            grad_q = grad_q + dot(ks[j][starts[s]], d_ref[span, :], TN)
        dqs[j][a] = (grad_q * scale).T.astype(BF16)

    def gather(b):
        first = TILES * NBR + b * TILES
        places = [places_ref[first + a] for a in range(TILES)]
        shares = [shares_ref[first + a] for a in range(TILES)]
        k_sum = dkc[places[0]] * shares[0]
        v_sum = dvc[places[0]] * shares[0]
        for a in range(1, TILES):
            k_sum = k_sum + dkc[places[a]] * shares[a]
            v_sum = v_sum + dvc[places[a]] * shares[a]
        return k_sum, v_sum

    def collect(j):
        def lower(i, _):
            k_sum, v_sum = gather(i)
            rim_out[j][0][i] = k_sum.astype(BF16)
            rim_out[j][1][i] = v_sum.astype(BF16)
            return 0

        def upper(i, _):
            k_sum, v_sum = gather(i + 2 * TILES)
            rim_out[j][2][i] = k_sum.astype(BF16)
            rim_out[j][3][i] = v_sum.astype(BF16)
            return 0

        def own(i, _):
            k_sum, v_sum = gather(i + TILES)
            own_k[j][i] = k_sum
            own_v[j][i] = v_sum
            return 0

        lax.fori_loop(0, TILES, lower, 0)
        lax.fori_loop(0, TILES, upper, 0)
        both(rim, j, "start")
        lax.fori_loop(0, TILES, own, 0)

    def combine(j):
        both(rim, j, "recv")

        def step(i, _):
            dks[j][i] = (
                own_k[j][i] + rim_in[j][0][i].astype(F32) + rim_in[j][2][i].astype(F32)
            ).astype(BF16)
            dvs[j][i] = (
                own_v[j][i] + rim_in[j][1][i].astype(F32) + rim_in[j][3][i].astype(F32)
            ).astype(BF16)
            return 0

        lax.fori_loop(0, TILES, step, 0)
        home(2, j, dks[j])
        home(3, j, dvs[j])

    for j in range(GROUP):
        spread(1, j, ks[j], TILES)
        spread(2, j, vs[j], TILES)
    for j in range(GROUP):
        spread(0, j, qs[j], 0)
        spread(3, j, gs[j], 0)

    blank = jnp.zeros((TILES, TILE, HD), BF16)
    for there, first in ((has_low, 0), (has_high, 2)):
        @pl.when(jnp.logical_not(there))
        def _():
            for j in range(GROUP):
                rim_in[j][first][...] = blank
                rim_in[j][first + 1][...] = blank
                ks[j][first * TILES:(first + 1) * TILES] = blank
                vs[j][first * TILES:(first + 1) * TILES] = blank

    for j in range(GROUP):
        arrived(1, j, ks[j], TILES)
        arrived(2, j, vs[j], TILES)
        both(halo, j, "start")
    for j in range(GROUP):
        arrived(0, j, qs[j], 0)
        arrived(3, j, gs[j], 0)
        both(halo, j, "recv")

        def step(a, _):
            attend(j, a)
            return 0

        lax.fori_loop(0, TILES, step, 0)
        home(0, j, os[j])
        home(1, j, dqs[j])
        collect(j)
        if j > 0:
            combine(j - 1)
    combine(GROUP - 1)

    for j in range(GROUP):
        both(halo, j, "send")
        both(rim, j, "send")
    for refs4, sems in ((args, send_in), (outs, send_out)):
        for a in range(4):
            @pl.when(has_self)
            def _():
                view = refs4[a].at[:, :, pl.ds(0, (groups - 1) * GROUP * HD)]
                pltpu.make_async_copy(view, view, sems.at[a]).wait()

            @pl.when(jnp.logical_not(has_self))
            def _():
                pltpu.make_async_copy(refs4[a], refs4[a], sems.at[a]).wait()
    for a in range(4):
        pltpu.make_async_copy(outs[a], outs[a], recv_out.at[a]).wait()


def tables(lists):
    tile, core = lax.axis_index("tile"), lax.axis_index("dp")
    swapped = lax.ppermute(lists, "dp", [(0, 1), (1, 0)])
    lists = jnp.where(core == tile % 2, lists, swapped)
    slab = 2 * (tile // 2) + core
    mine = lax.dynamic_slice_in_dim(lists, TILES * slab, TILES, 0)
    used = mine >= 0
    query = jnp.arange(TILES, dtype=jnp.int32)[:, None]
    local = jnp.where(used, mine - TILES * slab + TILES, TILES + query)
    match = jnp.logical_and(used, local == jnp.arange(3 * TILES, dtype=jnp.int32)[:, None, None])
    slot = jnp.max(jnp.where(match, jnp.arange(NBR, dtype=jnp.int32), 0), axis=2)
    places = jnp.concatenate([local.reshape(-1), (slot + NBR * query.T).reshape(-1)])
    hides = jnp.where(used, 0.0, 1e30).astype(F32)
    shares = jnp.concatenate([hides.reshape(-1), jnp.any(match, axis=2).astype(F32).reshape(-1)])
    return places, shares


def body(queries, keys, values, grad_out, neighbours):
    slabs, groups = lax.axis_size("tile"), lax.axis_size("head")
    rows = TILES * TILE
    places, shares = tables(neighbours[0])
    head = pltpu.VMEM((TILES, TILE, HD), BF16)
    wide = pltpu.VMEM((3 * TILES, TILE, HD), BF16)
    total = pltpu.VMEM((TILES, TILE, HD), F32)
    dma = pltpu.SemaphoreType.DMA
    scratch = (
        [head] * (2 * GROUP) + [wide] * (2 * GROUP) + [head] * (4 * GROUP) + [total] * (2 * GROUP)
        + [head] * (8 * GROUP)
        + [
            pltpu.VMEM((NBR * TILE, TILE), F32),
            pltpu.VMEM((NBR * TILE, TILE), BF16),
            pltpu.VMEM((NBR * TILE, TILE), BF16),
            pltpu.VMEM((TILES * NBR, TILE, HD), F32),
            pltpu.VMEM((TILES * NBR, TILE, HD), F32),
            dma((4,)), dma((4, GROUP)), dma((GROUP, 2, 2)), dma((GROUP, 2, 2)), dma((GROUP, 2, 2)),
            dma((GROUP, 2, 2)), dma((4,)), dma((4,)),
        ]
    )
    anywhere = pl.BlockSpec(memory_space=pl.ANY)
    shape = jax.ShapeDtypeStruct(queries.shape, BF16)
    return tuple(pl.pallas_call(
        functools.partial(kernel, slabs, groups),
        out_shape=(shape,) * 4,
        in_specs=[anywhere] * 4 + [pl.BlockSpec(memory_space=pltpu.SMEM)] * 2,
        out_specs=(anywhere,) * 4,
        scratch_shapes=scratch,
        compiler_params=pltpu.CompilerParams(
            collective_id=0, has_side_effects=True, vmem_limit_bytes=58 * 1024 * 1024
        ),
    )(queries, keys, values, grad_out, places, shares))


def solution(mesh):
    tokens = P("dp", ("tile", "head"), None)
    return jax.shard_map(
        body,
        mesh=mesh,
        in_specs=(tokens,) * 4 + (P("dp", None, None),),
        out_specs=(tokens,) * 4,
        check_vma=False,
    )
```

time: 852 us -> 130 us (0.15)
  the two profiles are of different devices: /device:TPU:6 before, /device:TPU:1 now
where the time goes in v1:
time: 130 us; the launch traced here: 129 us
  Pallas kernels  116 us (89%)
  local copies, waits for them, and re-layouts  7.7 us (6%)
  other arithmetic  2.28 us (2%)
  starting transfers between devices  1.5 us (1%)
    pallas_call x1, Pallas kernels, body(): pl.pallas_call(functools.partial(kernel, slabs, groups), out_shape=(shape...  116 us
    unnamed x10, local copies, waits for them, and re-layouts  6.86 us
  transfers between devices with their start and end apart: 1, of which 1 were waited for; matrix products, arithmetic and copies ran while one was open for 0% of the time, Pallas kernels for 0%

profile of v1, /device:TPU:1, one launch (start us, length us, event | category | flops | bytes accessed | tf_op | source)
XLA Modules:
  0.0 129.4 jit_solution(2997112581477240390)
XLA Ops:
  0.6 1.5 %collective-permute-start = (s32[32,4]{0,1:T(4,128)}, s32[32,4]{0,1:T(4,128)S(1)}, u32[]{:S(2)}, u32[]{:S(2)}) collective-permute-start(s32[32,4]{0,1:T(4,128)} %bitcast.2), channel_id=1, source_target_pairs={{0,1},{1,0},{2,3},{3,2},{4,5},{5,4},{6,7},{7,6},{8,9},{9,8},{10,11... | collective-permute-start | bytes 1544 | tf_op jit(solution)/shard_map/ppermute | solution.py:323
  2.1 1.0 collective-permute-done
  3.2 0.7 broadcast_select_fusion.1
  3.8 0.1 broadcast_select_fusion
  3.9 0.1 copy.18
  4.0 0.1 add_select_fusion
  4.1 0.1 copy.17
  4.2 0.1 reshape.34
  4.3 0.1 fusion.1
  4.4 0.1 select_reduce_fusion
  4.5 0.1 copy.21
  4.6 0.1 reshape.35
  4.7 0.1 copy.22
  4.8 0.1 reshape.36
  4.9 0.1 broadcast_add_fusion
  4.9 0.1 copy.20
  5.0 0.1 add.41
  5.1 0.6 pad_maximum_fusion.refs_5_
  5.7 0.6 pad_add_fusion.refs_4_
  6.3 116.3 %shard_map.84 = (bf16[1,192,3072]{2,1,0:T(8,128)(2,1)}, bf16[1,192,3072]{2,1,0:T(8,128)(2,1)}, bf16[1,192,3072]{2,1,0:T(8,128)(2,1)}, bf16[1,192,3072]{2,1,0:T(8,128)(2,1)}) custom-call(bf16[1,192,3072]{2,1,0:T(8,128)(2,1)} %refs_0_.1, bf16[1,192,3072]{2,1,0:T(8,128)(2,1)} %refs_1_.1, bf16[1,192,3072]{2,1,0:T(8,128)(2,1)} %refs_2_.1, ...), custom_call_target="tpu_custom_call" | custom-call | tf_op jit(solution)/shard_map/pallas_call | solution.py:361
  122.6 0.0 copy-start.2
  122.6 2.5 %copy.27 = bf16[1,192,3072]{2,1,0:T(8,128)(2,1)} copy(bf16[1,192,3072]{2,1,0:T(8,128)(2,1)} %get-tuple-element.10) | data formatting | bytes 2359296
  125.0 0.0 copy-done.2
  125.0 0.0 copy-start.1
  125.0 1.0 copy.28
  126.0 0.7 copy-done.1
  126.7 0.0 copy-start
  126.7 1.0 copy.29
  127.7 0.7 copy-done
  128.4 1.0 copy.30
  (3 shorter events, 0.0 us)
Async XLA Ops:
  0.6 2.5 %collective-permute-start = (s32[32,4]{0,1:T(4,128)}, s32[32,4]{0,1:T(4,128)S(1)}, u32[]{:S(2)}, u32[]{:S(2)}) collective-permute-start(s32[32,4]{0,1:T(4,128)} %bitcast.2), channel_id=1, source_target_pairs={{0,1},{1,0},{2,3},{3,2},{4,5},{5,4},{6,7},{7,6},{8,9},{9,8},{10,11... | collective-permute-start | bytes 1544 | tf_op jit(solution)/shard_map/ppermute | solution.py:323
  122.6 2.5 %copy-start.2 = (bf16[1,192,3072]{2,1,0:T(8,128)(2,1)S(1)}, bf16[1,192,3072]{2,1,0:T(8,128)(2,1)}, u32[]{:S(2)}) copy-start(bf16[1,192,3072]{2,1,0:T(8,128)(2,1)} %get-tuple-element.11) | copy-start | bytes 3538948
  125.0 1.7 %copy-start.1 = (bf16[1,192,3072]{2,1,0:T(8,128)(2,1)S(1)}, bf16[1,192,3072]{2,1,0:T(8,128)(2,1)}, u32[]{:S(2)}) copy-start(bf16[1,192,3072]{2,1,0:T(8,128)(2,1)} %get-tuple-element.12) | copy-start | bytes 3538948
  126.7 1.7 %copy-start = (bf16[1,192,3072]{2,1,0:T(8,128)(2,1)S(1)}, bf16[1,192,3072]{2,1,0:T(8,128)(2,1)}, u32[]{:S(2)}) copy-start(bf16[1,192,3072]{2,1,0:T(8,128)(2,1)} %get-tuple-element.13) | copy-start | bytes 3538948

commit v2 on v1

--- a/solution.py
+++ b/solution.py
@@ -27,8 +27,8 @@
 
 
 def kernel(slabs, groups, *refs):
-    args, places_ref, shares_ref, outs = refs[:4], refs[4], refs[5], refs[6:10]
-    it = iter(refs[10:])
+    args, lists, outs = refs[:4], refs[4], refs[5:9]
+    it = iter(refs[9:])
 
     def take(n):
         return [next(it) for _ in range(n)]
@@ -38,8 +38,8 @@
     own_k, own_v = take(GROUP), take(GROUP)
     rim_out = [take(4) for _ in range(GROUP)]
     rim_in = [take(4) for _ in range(GROUP)]
-    s_ref, e_ref, d_ref, dkc, dvc = take(5)
-    (send_in, recv_in, halo_send, halo_recv, rim_send, rim_recv, send_out, recv_out) = take(8)
+    s_ref, e_ref, d_ref, dkc, dvc, lists_both, lists_here, places_ref, shares_ref = take(9)
+    (send_in, recv_in, halo_send, halo_recv, rim_send, rim_recv, send_out, recv_out, list_sems) = take(9)
 
     tile = lax.axis_index("tile")
     group = lax.axis_index("head")
@@ -80,6 +80,39 @@
 
     count = groups - has_self.astype(jnp.int32) + has_low.astype(jnp.int32) + has_high.astype(jnp.int32)
     pl.semaphore_wait(barrier, count)
+
+    keep = pltpu.make_async_copy(lists, lists_both.at[core], list_sems.at[0])
+    give = pltpu.make_async_remote_copy(
+        src_ref=lists, dst_ref=lists_both.at[core], send_sem=list_sems.at[1], recv_sem=list_sems.at[2],
+        device_id=(tile, group, 1 - core), device_id_type=MESH,
+    )
+
+    def tabulate():
+        def entry(a, s):
+            return lists_here[0, (TILES * slab + a) * NBR + s]
+
+        def slots(a, _):
+            for s in range(NBR):
+                named = entry(a, s)
+                used = named >= 0
+                local = lax.min(lax.max(named - TILES * (slab - 1), 0), 3 * TILES - 1)
+                places_ref[a * NBR + s] = jnp.where(used, local, TILES + a)
+                shares_ref[a * NBR + s] = jnp.where(used, 0.0, 1e30).astype(F32)
+            return 0
+
+        def terms(b, _):
+            for a in range(TILES):
+                slot, share = jnp.int32(0), jnp.float32(0)
+                for s in range(NBR):
+                    match = entry(a, s) == TILES * (slab - 1) + b
+                    slot = jnp.where(match, s, slot)
+                    share = jnp.where(match, 1.0, share)
+                places_ref[TILES * NBR + b * TILES + a] = a * NBR + slot
+                shares_ref[TILES * NBR + b * TILES + a] = share
+            return 0
+
+        lax.fori_loop(0, TILES, slots, 0)
+        lax.fori_loop(0, 3 * TILES, terms, 0)
 
     def spread(a, j, dst, offset):
         def step(i, _):
@@ -266,9 +299,11 @@
     for j in range(GROUP):
         spread(1, j, ks[j], TILES)
         spread(2, j, vs[j], TILES)
-    for j in range(GROUP):
         spread(0, j, qs[j], 0)
         spread(3, j, gs[j], 0)
+        if j == 0:
+            keep.start()
+            give.start()
 
     blank = jnp.zeros((TILES, TILE, HD), BF16)
     for there, first in ((has_low, 0), (has_high, 2)):
@@ -280,10 +315,19 @@
                 ks[j][first * TILES:(first + 1) * TILES] = blank
                 vs[j][first * TILES:(first + 1) * TILES] = blank
 
-    for j in range(GROUP):
+    keep.wait()
+    give.wait()
+    down = pltpu.make_async_copy(lists_both.at[side], lists_here, list_sems.at[3])
+    down.start()
+    down.wait()
+    tabulate()
+
+    def pass_on(j):
         arrived(1, j, ks[j], TILES)
         arrived(2, j, vs[j], TILES)
         both(halo, j, "start")
+
+    pass_on(0)
     for j in range(GROUP):
         arrived(0, j, qs[j], 0)
         arrived(3, j, gs[j], 0)
@@ -291,14 +335,20 @@
 
         def step(a, _):
             attend(j, a)
+
+            @pl.when(a == TILES // 2)
+            def _():
+                if j < GROUP - 1:
+                    pass_on(j + 1)
+                if j > 0:
+                    combine(j - 1)
+
             return 0
 
         lax.fori_loop(0, TILES, step, 0)
         home(0, j, os[j])
         home(1, j, dqs[j])
         collect(j)
-        if j > 0:
-            combine(j - 1)
     combine(GROUP - 1)
 
     for j in range(GROUP):
@@ -318,27 +368,32 @@
         pltpu.make_async_copy(outs[a], outs[a], recv_out.at[a]).wait()
 
 
-def tables(lists):
-    tile, core = lax.axis_index("tile"), lax.axis_index("dp")
-    swapped = lax.ppermute(lists, "dp", [(0, 1), (1, 0)])
-    lists = jnp.where(core == tile % 2, lists, swapped)
-    slab = 2 * (tile // 2) + core
-    mine = lax.dynamic_slice_in_dim(lists, TILES * slab, TILES, 0)
-    used = mine >= 0
-    query = jnp.arange(TILES, dtype=jnp.int32)[:, None]
-    local = jnp.where(used, mine - TILES * slab + TILES, TILES + query)
-    match = jnp.logical_and(used, local == jnp.arange(3 * TILES, dtype=jnp.int32)[:, None, None])
-    slot = jnp.max(jnp.where(match, jnp.arange(NBR, dtype=jnp.int32), 0), axis=2)
-    places = jnp.concatenate([local.reshape(-1), (slot + NBR * query.T).reshape(-1)])
-    hides = jnp.where(used, 0.0, 1e30).astype(F32)
-    shares = jnp.concatenate([hides.reshape(-1), jnp.any(match, axis=2).astype(F32).reshape(-1)])
-    return places, shares
+def settle(*refs):
+    given, kept, held, sems = refs[:4], refs[4:8], refs[8], refs[9]
+    parts = sems.shape[2]
+    size = given[0].shape[1] // parts
+    pairs = []
+    for i in range(parts):
+        for a in range(4):
+            rows = pl.ds(i * size, size)
+            pairs.append((
+                pltpu.make_async_copy(given[a].at[0, rows, :], held.at[a, rows, :], sems.at[0, a, i]),
+                pltpu.make_async_copy(held.at[a, rows, :], kept[a].at[0, rows, :], sems.at[1, a, i]),
+            ))
+    for into, _ in pairs:
+        into.start()
+    for into, out in pairs:
+        into.wait()
+        out.start()
+    for _, out in pairs:
+        out.wait()
 
 
 def body(queries, keys, values, grad_out, neighbours):
     slabs, groups = lax.axis_size("tile"), lax.axis_size("head")
     rows = TILES * TILE
-    places, shares = tables(neighbours[0])
+    lists = neighbours.reshape(-1)
+    lists = jnp.pad(lists, (0, 8 * 128 - lists.shape[0])).reshape(8, 128)
     head = pltpu.VMEM((TILES, TILE, HD), BF16)
     wide = pltpu.VMEM((3 * TILES, TILE, HD), BF16)
     total = pltpu.VMEM((TILES, TILE, HD), F32)
@@ -352,22 +407,33 @@
             pltpu.VMEM((NBR * TILE, TILE), BF16),
             pltpu.VMEM((TILES * NBR, TILE, HD), F32),
             pltpu.VMEM((TILES * NBR, TILE, HD), F32),
+            pltpu.VMEM((2, 8, 128), jnp.int32),
+            pltpu.SMEM((8, 128), jnp.int32),
+            pltpu.SMEM((TILES * NBR + 3 * TILES * TILES,), jnp.int32),
+            pltpu.SMEM((TILES * NBR + 3 * TILES * TILES,), F32),
             dma((4,)), dma((4, GROUP)), dma((GROUP, 2, 2)), dma((GROUP, 2, 2)), dma((GROUP, 2, 2)),
-            dma((GROUP, 2, 2)), dma((4,)), dma((4,)),
+            dma((GROUP, 2, 2)), dma((4,)), dma((4,)), dma((4,)),
         ]
     )
     anywhere = pl.BlockSpec(memory_space=pl.ANY)
     shape = jax.ShapeDtypeStruct(queries.shape, BF16)
-    return tuple(pl.pallas_call(
+    results = pl.pallas_call(
         functools.partial(kernel, slabs, groups),
         out_shape=(shape,) * 4,
-        in_specs=[anywhere] * 4 + [pl.BlockSpec(memory_space=pltpu.SMEM)] * 2,
+        in_specs=[anywhere] * 5,
         out_specs=(anywhere,) * 4,
         scratch_shapes=scratch,
         compiler_params=pltpu.CompilerParams(
             collective_id=0, has_side_effects=True, vmem_limit_bytes=58 * 1024 * 1024
         ),
-    )(queries, keys, values, grad_out, places, shares))
+    )(queries, keys, values, grad_out, lists)
+    return tuple(pl.pallas_call(
+        settle,
+        out_shape=(shape,) * 4,
+        in_specs=[anywhere] * 4,
+        out_specs=(anywhere,) * 4,
+        scratch_shapes=[pltpu.VMEM((4,) + queries.shape[1:], BF16), dma((2, 4, 4))],
+    )(*results))
 
 
 def solution(mesh):

time: 130 us -> 117 us (0.900)
  local copies, waits for them, and re-layouts: 7.7 us -> 1.47 us
  other arithmetic: 2.28 us -> 0 us
  starting transfers between devices: 1.5 us -> 0 us
    unnamed x10 -> x1, local copies, waits for them, and re-layouts: 6.86 us -> 0.76 us
    pallas_call x1, Pallas kernels: 116 us -> 110 us  [body(): pl.pallas_call(functools.partial(kernel, slabs, groups), out_shape=(shape...]
    pallas_call x0 -> x1, Pallas kernels: none -> 4.38 us  [body(): pl.pallas_call(settle, out_shape=(shape,) * 4, in_specs=[anywhere] * 4, o...]
    ppermute x1 -> x0, starting transfers between devices: 1.5 us -> none  [tables(): swapped = lax.ppermute(lists, 'dp', [(0, 1), (1, 0)])]
  transfers between devices with their start and end apart: 1 -> 0, of which waited for: 1 -> 0; matrix products, arithmetic and copies ran while one was open for 0% -> 0% of each run, Pallas kernels for 0% -> 0%
where the time goes in v2:
time: 117 us
  Pallas kernels  115 us (98%)
  local copies, waits for them, and re-layouts  1.47 us (1%)
    pallas_call x1, Pallas kernels, body(): pl.pallas_call(functools.partial(kernel, slabs, groups), out_shape=(shape...  110 us
    pallas_call x1, Pallas kernels, body(): pl.pallas_call(settle, out_shape=(shape,) * 4, in_specs=[anywhere] * 4, o...  4.38 us

profile of v2, /device:TPU:1, one launch (start us, length us, event | category | flops | bytes accessed | tf_op | source)
XLA Modules:
  0.0 116.8 jit_solution(6740346428006273292)
XLA Ops:
  0.6 0.8 copy.10
  1.4 0.1 reshape.14
  1.5 0.6 pad_bitcast_fusion.refs_4_
  2.1 110.4 %shard_map.84 = (bf16[1,192,3072]{2,1,0:T(8,128)(2,1)}, bf16[1,192,3072]{2,1,0:T(8,128)(2,1)}, bf16[1,192,3072]{2,1,0:T(8,128)(2,1)}, bf16[1,192,3072]{2,1,0:T(8,128)(2,1)}) custom-call(bf16[1,192,3072]{2,1,0:T(8,128)(2,1)} %refs_0_.1, bf16[1,192,3072]{2,1,0:T(8,128)(2,1)} %refs_1_.1, bf16[1,192,3072]{2,1,0:T(8,128)(2,1)} %refs_2_.1, ...), custom_call_target="tpu_custom_call" | custom-call | tf_op jit(solution)/shard_map/pallas_call | solution.py:420
  112.5 4.4 %shard_map.85 = (bf16[1,192,3072]{2,1,0:T(8,128)(2,1)}, bf16[1,192,3072]{2,1,0:T(8,128)(2,1)}, bf16[1,192,3072]{2,1,0:T(8,128)(2,1)}, bf16[1,192,3072]{2,1,0:T(8,128)(2,1)}) custom-call(bf16[1,192,3072]{2,1,0:T(8,128)(2,1)} %get-tuple-element.8.refs_0_, bf16[1,192,3072]{2,1,0:T(8,128)(2,1)} %get-tuple-element.9.refs_1_, ...), custom_call_target="tpu_custom_call" | custom-call | tf_op jit(solution)/shard_map/pallas_call | solution.py:430

commit v3 on v2

--- a/solution.py
+++ b/solution.py
@@ -89,7 +89,7 @@
 
     def tabulate():
         def entry(a, s):
-            return lists_here[0, (TILES * slab + a) * NBR + s]
+            return lists_here[s, TILES * slab + a]
 
         def slots(a, _):
             for s in range(NBR):
@@ -114,24 +114,27 @@
         lax.fori_loop(0, TILES, slots, 0)
         lax.fori_loop(0, 3 * TILES, terms, 0)
 
-    def spread(a, j, dst, offset):
+    def deliver(src, to, g, sent, landed):
+        here = jnp.logical_and(has_self, g == group)
+
+        @pl.when(here)
+        def _():
+            pltpu.make_async_copy(src, to, landed).start()
+
+        @pl.when(jnp.logical_not(here))
+        def _():
+            pltpu.make_async_remote_copy(
+                src_ref=src, dst_ref=to, send_sem=sent, recv_sem=landed,
+                device_id=(column[0], g, column[1]), device_id_type=MESH,
+            ).start()
+
+    def spread(*moves):
         def step(i, _):
-            g = (group + i) % groups
-            src = args[a].at[0, :, pl.ds(pl.multiple_of((g * GROUP + j) * HD, HD), HD)]
-            to = dst.at[offset + group * block // TILE, pl.ds(pl.multiple_of(group * block % TILE, block), block), :]
-            here = jnp.logical_and(has_self, g == group)
-
-            @pl.when(here)
-            def _():
-                pltpu.make_async_copy(src, to, recv_in.at[a, j]).start()
-
-            @pl.when(jnp.logical_not(here))
-            def _():
-                pltpu.make_async_remote_copy(
-                    src_ref=src, dst_ref=to, send_sem=send_in.at[a], recv_sem=recv_in.at[a, j],
-                    device_id=(column[0], g, column[1]), device_id_type=MESH,
-                ).start()
-
+            for n, (a, j, dst, offset) in enumerate(moves):
+                g = (group + i + n * groups // len(moves)) % groups
+                src = args[a].at[0, :, pl.ds(pl.multiple_of((g * GROUP + j) * HD, HD), HD)]
+                to = dst.at[offset + group * block // TILE, pl.ds(pl.multiple_of(group * block % TILE, block), block), :]
+                deliver(src, to, g, send_in.at[a], recv_in.at[a, j])
             return 0
 
         lax.fori_loop(0, groups, step, 0)
@@ -140,24 +143,13 @@
         view = dst.at[pl.ds(offset, TILES)]
         pltpu.make_async_copy(view, view, recv_in.at[a, j]).wait()
 
-    def home(a, j, src):
+    def home(*moves):
         def step(i, _):
-            g = (group + i) % groups
-            piece = src.at[g * block // TILE, pl.ds(pl.multiple_of(g * block % TILE, block), block), :]
-            to = outs[a].at[0, :, pl.ds(pl.multiple_of((group * GROUP + j) * HD, HD), HD)]
-            here = jnp.logical_and(has_self, g == group)
-
-            @pl.when(here)
-            def _():
-                pltpu.make_async_copy(piece, to, recv_out.at[a]).start()
-
-            @pl.when(jnp.logical_not(here))
-            def _():
-                pltpu.make_async_remote_copy(
-                    src_ref=piece, dst_ref=to, send_sem=send_out.at[a], recv_sem=recv_out.at[a],
-                    device_id=(column[0], g, column[1]), device_id_type=MESH,
-                ).start()
-
+            for n, (a, j, src) in enumerate(moves):
+                g = (group + i + n * groups // len(moves)) % groups
+                piece = src.at[g * block // TILE, pl.ds(pl.multiple_of(g * block % TILE, block), block), :]
+                to = outs[a].at[0, :, pl.ds(pl.multiple_of((group * GROUP + j) * HD, HD), HD)]
+                deliver(piece, to, g, send_out.at[a], recv_out.at[a])
             return 0
 
         lax.fori_loop(0, groups, step, 0)
@@ -293,14 +285,11 @@
             return 0
 
         lax.fori_loop(0, TILES, step, 0)
-        home(2, j, dks[j])
-        home(3, j, dvs[j])
+        home((2, j, dks[j]), (3, j, dvs[j]))
 
     for j in range(GROUP):
-        spread(1, j, ks[j], TILES)
-        spread(2, j, vs[j], TILES)
-        spread(0, j, qs[j], 0)
-        spread(3, j, gs[j], 0)
+        spread((1, j, ks[j], TILES), (2, j, vs[j], TILES))
+        spread((0, j, qs[j], 0), (3, j, gs[j], 0))
         if j == 0:
             keep.start()
             give.start()
@@ -346,8 +335,7 @@
             return 0
 
         lax.fori_loop(0, TILES, step, 0)
-        home(0, j, os[j])
-        home(1, j, dqs[j])
+        home((0, j, os[j]), (1, j, dqs[j]))
         collect(j)
     combine(GROUP - 1)
 
@@ -369,31 +357,24 @@
 
 
 def settle(*refs):
-    given, kept, held, sems = refs[:4], refs[4:8], refs[8], refs[9]
-    parts = sems.shape[2]
+    given, kept, sems = refs[:4], refs[4:8], refs[8]
+    parts = sems.shape[1]
     size = given[0].shape[1] // parts
-    pairs = []
+    copies = []
     for i in range(parts):
         for a in range(4):
             rows = pl.ds(i * size, size)
-            pairs.append((
-                pltpu.make_async_copy(given[a].at[0, rows, :], held.at[a, rows, :], sems.at[0, a, i]),
-                pltpu.make_async_copy(held.at[a, rows, :], kept[a].at[0, rows, :], sems.at[1, a, i]),
-            ))
-    for into, _ in pairs:
-        into.start()
-    for into, out in pairs:
-        into.wait()
-        out.start()
-    for _, out in pairs:
-        out.wait()
+            copies.append(pltpu.make_async_copy(given[a].at[0, rows, :], kept[a].at[0, rows, :], sems.at[a, i]))
+    for copy in copies:
+        copy.start()
+    for copy in copies:
+        copy.wait()
 
 
 def body(queries, keys, values, grad_out, neighbours):
     slabs, groups = lax.axis_size("tile"), lax.axis_size("head")
     rows = TILES * TILE
-    lists = neighbours.reshape(-1)
-    lists = jnp.pad(lists, (0, 8 * 128 - lists.shape[0])).reshape(8, 128)
+    lists = neighbours[0].T
     head = pltpu.VMEM((TILES, TILE, HD), BF16)
     wide = pltpu.VMEM((3 * TILES, TILE, HD), BF16)
     total = pltpu.VMEM((TILES, TILE, HD), F32)
@@ -407,8 +388,8 @@
             pltpu.VMEM((NBR * TILE, TILE), BF16),
             pltpu.VMEM((TILES * NBR, TILE, HD), F32),
             pltpu.VMEM((TILES * NBR, TILE, HD), F32),
-            pltpu.VMEM((2, 8, 128), jnp.int32),
-            pltpu.SMEM((8, 128), jnp.int32),
+            pltpu.VMEM((2,) + lists.shape, jnp.int32),
+            pltpu.SMEM(lists.shape, jnp.int32),
             pltpu.SMEM((TILES * NBR + 3 * TILES * TILES,), jnp.int32),
             pltpu.SMEM((TILES * NBR + 3 * TILES * TILES,), F32),
             dma((4,)), dma((4, GROUP)), dma((GROUP, 2, 2)), dma((GROUP, 2, 2)), dma((GROUP, 2, 2)),
@@ -419,20 +400,22 @@
     shape = jax.ShapeDtypeStruct(queries.shape, BF16)
     results = pl.pallas_call(
         functools.partial(kernel, slabs, groups),
-        out_shape=(shape,) * 4,
+        out_shape=(pltpu.VMEM(queries.shape, BF16),) * 4,
         in_specs=[anywhere] * 5,
         out_specs=(anywhere,) * 4,
         scratch_shapes=scratch,
         compiler_params=pltpu.CompilerParams(
-            collective_id=0, has_side_effects=True, vmem_limit_bytes=58 * 1024 * 1024
+            collective_id=0, has_side_effects=True, vmem_limit_bytes=54 * 1024 * 1024
         ),
-    )(queries, keys, values, grad_out, lists)
+    )(*(pltpu.with_memory_space_constraint(x, pltpu.HBM) for x in (queries, keys, values, grad_out)), lists)
+    results = [pltpu.with_memory_space_constraint(r, pltpu.VMEM) for r in results]
     return tuple(pl.pallas_call(
         settle,
         out_shape=(shape,) * 4,
-        in_specs=[anywhere] * 4,
+        in_specs=[pl.BlockSpec(memory_space=pltpu.VMEM)] * 4,
         out_specs=(anywhere,) * 4,
-        scratch_shapes=[pltpu.VMEM((4,) + queries.shape[1:], BF16), dma((2, 4, 4))],
+        scratch_shapes=[dma((4, 1))],
+        compiler_params=pltpu.CompilerParams(vmem_limit_bytes=4 * 1024 * 1024),
     )(*results))
 
 

time: 117 us -> 114 us (0.974)
  Pallas kernels: 115 us -> 113 us
  local copies, waits for them, and re-layouts: 1.47 us -> 0 us
    pallas_call x2, Pallas kernels: 115 us -> 113 us  [the longest x1 111 us: body(): pl.pallas_call(functools.partial(kernel, slabs, groups), out_shape=(pltpu...]
where the time goes in v3:
time: 114 us
  Pallas kernels  113 us (99%)
    pallas_call x1, Pallas kernels, body(): pl.pallas_call(functools.partial(kernel, slabs, groups), out_shape=(pltpu...  111 us

profile of v3, /device:TPU:1, one launch (start us, length us, event | category | flops | bytes accessed | tf_op | source)
XLA Modules:
  0.0 113.8 jit_solution(2871463661350054343)
XLA Ops:
  0.6 110.9 %shard_map.84 = (bf16[1,192,3072]{2,1,0:T(8,128)(2,1)S(1)}, bf16[1,192,3072]{2,1,0:T(8,128)(2,1)S(1)}, bf16[1,192,3072]{2,1,0:T(8,128)(2,1)S(1)}, bf16[1,192,3072]{2,1,0:T(8,128)(2,1)S(1)}) custom-call(bf16[1,192,3072]{2,1,0:T(8,128)(2,1)} %refs_0_.1, bf16[1,192,3072]{2,1,0:T(8,128)(2,1)} %refs_1_.1, bf16[1,192,3072]{2,1,0:T(8,128)(2,1)} %refs_2_.1, ...), custom_call_target="tpu_custom_call" | custom-call | tf_op jit(solution)/shard_map/pallas_call | solution.py:401
  111.6 2.2 %shard_map.85 = (bf16[1,192,3072]{2,1,0:T(8,128)(2,1)}, bf16[1,192,3072]{2,1,0:T(8,128)(2,1)}, bf16[1,192,3072]{2,1,0:T(8,128)(2,1)}, bf16[1,192,3072]{2,1,0:T(8,128)(2,1)}) custom-call(bf16[1,192,3072]{2,1,0:T(8,128)(2,1)S(1)} %get-tuple-element.8.refs_0_, bf16[1,192,3072]{2,1,0:T(8,128)(2,1)S(1)} %get-tuple-element.9.refs_1_, ...), custom_call_target="tpu_custom_call" | custom-call | tf_op jit(solution)/shard_map/pallas_call | solution.py:412

commit v4 on v3

--- a/solution.py
+++ b/solution.py
@@ -131,7 +131,7 @@
     def spread(*moves):
         def step(i, _):
             for n, (a, j, dst, offset) in enumerate(moves):
-                g = (group + i + n * groups // len(moves)) % groups
+                g = (group + n * groups // len(moves) + i * (1 - 2 * core) + groups) % groups
                 src = args[a].at[0, :, pl.ds(pl.multiple_of((g * GROUP + j) * HD, HD), HD)]
                 to = dst.at[offset + group * block // TILE, pl.ds(pl.multiple_of(group * block % TILE, block), block), :]
                 deliver(src, to, g, send_in.at[a], recv_in.at[a, j])
@@ -146,7 +146,7 @@
     def home(*moves):
         def step(i, _):
             for n, (a, j, src) in enumerate(moves):
-                g = (group + i + n * groups // len(moves)) % groups
+                g = (group + n * groups // len(moves) + i * (1 - 2 * core) + groups) % groups
                 piece = src.at[g * block // TILE, pl.ds(pl.multiple_of(g * block % TILE, block), block), :]
                 to = outs[a].at[0, :, pl.ds(pl.multiple_of((group * GROUP + j) * HD, HD), HD)]
                 deliver(piece, to, g, send_out.at[a], recv_out.at[a])
@@ -270,6 +270,7 @@
         lax.fori_loop(0, TILES, lower, 0)
         lax.fori_loop(0, TILES, upper, 0)
         both(rim, j, "start")
+        home((0, j, os[j]), (1, j, dqs[j]))
         lax.fori_loop(0, TILES, own, 0)
 
     def combine(j):
@@ -335,7 +336,6 @@
             return 0
 
         lax.fori_loop(0, TILES, step, 0)
-        home((0, j, os[j]), (1, j, dqs[j]))
         collect(j)
     combine(GROUP - 1)
 

time: 114 us -> 114 us (level)
  no operation moved by 1% of the time
where the time goes in v4:
time: 114 us
  Pallas kernels  113 us (99%)
    pallas_call x1, Pallas kernels, body(): pl.pallas_call(functools.partial(kernel, slabs, groups), out_shape=(pltpu...  111 us

profile of v4, /device:TPU:1, one launch (start us, length us, event | category | flops | bytes accessed | tf_op | source)
XLA Modules:
  0.0 113.8 jit_solution(1428153718830459865)
XLA Ops:
  0.6 110.9 %shard_map.84 = (bf16[1,192,3072]{2,1,0:T(8,128)(2,1)S(1)}, bf16[1,192,3072]{2,1,0:T(8,128)(2,1)S(1)}, bf16[1,192,3072]{2,1,0:T(8,128)(2,1)S(1)}, bf16[1,192,3072]{2,1,0:T(8,128)(2,1)S(1)}) custom-call(bf16[1,192,3072]{2,1,0:T(8,128)(2,1)} %refs_0_.1, bf16[1,192,3072]{2,1,0:T(8,128)(2,1)} %refs_1_.1, bf16[1,192,3072]{2,1,0:T(8,128)(2,1)} %refs_2_.1, ...), custom_call_target="tpu_custom_call" | custom-call | tf_op jit(solution)/shard_map/pallas_call | solution.py:401
  111.6 2.2 %shard_map.85 = (bf16[1,192,3072]{2,1,0:T(8,128)(2,1)}, bf16[1,192,3072]{2,1,0:T(8,128)(2,1)}, bf16[1,192,3072]{2,1,0:T(8,128)(2,1)}, bf16[1,192,3072]{2,1,0:T(8,128)(2,1)}) custom-call(bf16[1,192,3072]{2,1,0:T(8,128)(2,1)S(1)} %get-tuple-element.8.refs_0_, bf16[1,192,3072]{2,1,0:T(8,128)(2,1)S(1)} %get-tuple-element.9.refs_1_, ...), custom_call_target="tpu_custom_call" | custom-call | tf_op jit(solution)/shard_map/pallas_call | solution.py:412

commit v5 on v3

--- a/solution.py
+++ b/solution.py
@@ -68,8 +68,6 @@
 
         return 0
 
-    lax.fori_loop(0, groups, greet, 0)
-
     @pl.when(has_low)
     def _():
         pl.semaphore_signal(barrier, inc=1, device_id=low_id, device_id_type=MESH)
@@ -77,6 +75,9 @@
     @pl.when(has_high)
     def _():
         pl.semaphore_signal(barrier, inc=1, device_id=high_id, device_id_type=MESH)
+
+    for i in range(groups):
+        greet((i + 1) % groups, 0)
 
     count = groups - has_self.astype(jnp.int32) + has_low.astype(jnp.int32) + has_high.astype(jnp.int32)
     pl.semaphore_wait(barrier, count)

time: 114 us -> 114 us (level)
  no operation moved by 1% of the time
where the time goes in v5:
time: 114 us
  Pallas kernels  113 us (99%)
    pallas_call x1, Pallas kernels, body(): pl.pallas_call(functools.partial(kernel, slabs, groups), out_shape=(pltpu...  111 us

profile of v5, /device:TPU:1, one launch (start us, length us, event | category | flops | bytes accessed | tf_op | source)
XLA Modules:
  0.0 113.8 jit_solution(5513381589932215074)
XLA Ops:
  0.6 110.9 %shard_map.84 = (bf16[1,192,3072]{2,1,0:T(8,128)(2,1)S(1)}, bf16[1,192,3072]{2,1,0:T(8,128)(2,1)S(1)}, bf16[1,192,3072]{2,1,0:T(8,128)(2,1)S(1)}, bf16[1,192,3072]{2,1,0:T(8,128)(2,1)S(1)}) custom-call(bf16[1,192,3072]{2,1,0:T(8,128)(2,1)} %refs_0_.1, bf16[1,192,3072]{2,1,0:T(8,128)(2,1)} %refs_1_.1, bf16[1,192,3072]{2,1,0:T(8,128)(2,1)} %refs_2_.1, ...), custom_call_target="tpu_custom_call" | custom-call | tf_op jit(solution)/shard_map/pallas_call | solution.py:402
  111.6 2.2 %shard_map.85 = (bf16[1,192,3072]{2,1,0:T(8,128)(2,1)}, bf16[1,192,3072]{2,1,0:T(8,128)(2,1)}, bf16[1,192,3072]{2,1,0:T(8,128)(2,1)}, bf16[1,192,3072]{2,1,0:T(8,128)(2,1)}) custom-call(bf16[1,192,3072]{2,1,0:T(8,128)(2,1)S(1)} %get-tuple-element.8.refs_0_, bf16[1,192,3072]{2,1,0:T(8,128)(2,1)S(1)} %get-tuple-element.9.refs_1_, ...), custom_call_target="tpu_custom_call" | custom-call | tf_op jit(solution)/shard_map/pallas_call | solution.py:413
